TPU v7x, 256 devices: a whole 4x4x8 slice. The times are simulated.
256 devices in a mesh: front: 64 (over z, y, core), rhs: 4 (over x).
Axes of the slice: x: 4, y: 4, z: 8, core: 2. Of those that a mesh axis runs over, the one named last changes fastest.
Arguments:
- right_side: float32 [32, 4, 8192], P('rhs', None, 'front'), may hold values from -6 to 6
- inverse_top: float32 [8192, 8192], P('front'), as said below
- inverse_second: float32 [8192, 4096], P('front'), as said below
- inverse_third: float32 [8192, 2048], P('front'), as said below
- inverse_fourth: float32 [8192, 1024], P('front'), as said below
- panels: float32 [3, 1024, 8192], P(None, None, 'front'), may hold values from -0.09375 to 0.09375
- targets: int32 [3, 64, 8], P(None, 'front'), may hold values from -1 to 191, as said below
Outputs:
- forward_result: float32 [32, 4, 8192], P('rhs', None, 'front')
- solution: float32 [32, 4, 8192], P('rhs', None, 'front')
Inputs may be any that keep to these rules, and one draw needn't show every extreme that they name: `targets`: for tier k + 1 the devices of one front hold the same list; its live entries are distinct blocks of that front's ancestors in the window (tiers 0 to k, the blocks inside the ancestor's devices), -1 marks an unused slot, each front has 1 to 8 live entries, and on every tier some front has exactly 8. `inverse_top`: within each front of D * 128 rows, with r the row's place in the front, the block is triangular in the elimination order o(r) = (r % 128) * D + r // 128: entry (i, j) is zero when o(j) > o(i); diagonal entries in 1 to 2. `inverse_second`: triangular in the same elimination order within each front, diagonal entries in 1 to 2. `inverse_third`: triangular in the same elimination order within each front, diagonal entries in 1 to 2. `inverse_fourth`: triangular in the same elimination order within each front, diagonal entries in 1 to 2.
All inputs are finite; a program needn't handle non-finite values.
Results may differ from a plain program's by a relative error of at most 0.0001.
Values sent between devices are 32-bit elements; how exact they have to be, the bound alone decides.
A program may use at most 64 MiB of HBM per device.

v0:
```python
import functools

import jax
import jax.numpy as jnp
from jax import lax
from jax.experimental import pallas as pl
from jax.experimental.pallas import tpu as pltpu
from jax.sharding import PartitionSpec as P

F32 = jnp.float32
BF16 = jnp.bfloat16
I32 = jnp.int32
MESH = pl.DeviceIdType.MESH
TIERS = 4
SLOTS = 8
BLOCKS = (64, 32, 16, 8)
PLANES = (8, 4, 2, 1)
TRANSPOSED = (((1,), (1,)), ((), ()))
NATURAL = (((1,), (0,)), ((), ()))


def split_rows(value):
    high = value.astype(BF16).astype(F32)
    return jnp.concatenate([high, value - high], axis=0).astype(BF16)


def fold_rows(value):
    return value[:8] + value[8:]


def fold_all(value):
    rows = fold_rows(value)
    sums = [
        rows[:, i : i + 128] + rows[:, i + 128 : i + 256] for i in range(0, rows.shape[1], 256)
    ]
    return sums[0] if len(sums) == 1 else jnp.concatenate(sums, axis=1)


def doubled(value):
    halves = split_rows(value)
    parts = [halves[:, i : i + 128] for i in range(0, halves.shape[1], 128)]
    return jnp.concatenate([part for part in parts for _ in range(2)], axis=1)


def matmul(left, right, dims):
    return lax.dot_general(left, right, dims, preferred_element_type=F32)


class Stage:
    def __init__(self):
        self.count = 0

    def take(self):
        self.count += 1
        return self.count - 1


STAGE_COUNT = 56

SCRATCH = dict(
    v0=((128, 8192), F32), v1=((128, 4096), F32), v2=((128, 2048), F32), v3=((128, 1024), F32),
    vp=((3, 1024, 128), F32),
    w0=((128, 8192), F32), w1=((128, 4096), F32), w2=((128, 2048), F32), wp=((2, 1024, 128), F32),
    c0=((64, 512, 128), BF16), c1=((32, 512, 128), BF16), c2=((16, 512, 128), BF16), c3=((8, 256, 128), BF16),
    pc3=((1024, 256), BF16), pc2=((1024, 512), BF16), pc1=((1024, 512), BF16),
    rb0=((8, 4, 2, 8, 128), F32), rb1=((4, 4, 2, 8, 128), F32), rb2=((2, 4, 2, 8, 128), F32), rb3=((1, 4, 2, 8, 128), F32),
    tgv=((8, 8, 128), I32),
    up3=((4, 2, 8, 128), F32), up2=((4, 2, 8, 128), F32), up1=((4, 2, 8, 128), F32),
    ur3=((8, 2, 8, 128), F32), ur2=((4, 2, 8, 128), F32), ur1=((4, 2, 8, 128), F32),
    us3=((2, 8, 128), F32), us2=((2, 8, 128), F32), us1=((2, 8, 128), F32),
    uz3=((8, 2, 8, 128), F32), uz2=((4, 2, 8, 128), F32), uz2b=((4, 2, 8, 128), F32), uz1=((8, 2, 8, 128), F32),
    s3p=((2, 8, 8, 128), F32), s3q=((2, 8, 8, 128), F32), s3r=((4, 8, 8, 128), F32),
    s2p=((2, 8, 8, 128), F32), s2q=((2, 8, 8, 128), F32), s1p=((2, 8, 8, 128), F32),
    st2=((2, 2, 8, 128), F32), st2b=((2, 2, 8, 128), F32), st1=((2, 2, 8, 128), F32),
    a1=((4, 2, 2, 8, 128), F32), a2=((4, 2, 2, 8, 128), F32), a3=((4, 2, 2, 8, 128), F32),
    ar1=((4, 2, 2, 8, 128), F32), ar2=((4, 2, 2, 8, 128), F32), ar3=((4, 2, 2, 8, 128), F32),
    as1=((2, 2, 8, 128), F32), as2=((2, 2, 8, 128), F32), as3=((2, 2, 8, 128), F32),
    az1=((8, 2, 8, 128), F32), az2=((4, 2, 8, 128), F32),
    pt1=((2, 8, 128), F32), pt2=((2, 8, 128), F32),
    pk1=((8, 8, 128), F32), pk2=((8, 8, 128), F32), pk3=((2, 8, 8, 128), F32),
    n0=((4, 12, 2, 8, 128), F32), nr0=((4, 12, 2, 8, 128), F32), ns0=((8, 2, 2, 8, 128), F32), nz0=((8, 2, 2, 8, 128), F32),
    n1=((4, 4, 2, 8, 128), F32), nr1=((4, 4, 2, 8, 128), F32), ns1=((4, 2, 8, 128), F32), nz1=((4, 2, 8, 128), F32),
    t0p=((2, 2, 8, 128), F32), t1p=((2, 8, 128), F32),
    sd0=((4, 8, 2, 8, 128), F32), sd1=((4, 4, 2, 8, 128), F32), sd2=((4, 2, 2, 8, 128), F32), sd3=((4, 1, 2, 8, 128), F32),
    dr0=((4, 8, 2, 8, 128), F32), dr1=((4, 4, 2, 8, 128), F32), dr2=((8, 2, 8, 128), F32), dr3=((8, 8, 128), F32),
    ds0=((8, 2, 8, 128), F32), ds1=((4, 2, 8, 128), F32),
    dz0=((8, 2, 8, 128), F32), dz1=((4, 2, 8, 128), F32),
    fk=((3, 8, 256), F32), fout=((3, 8, 128), F32), fin=((3, 8, 128), F32), sout=((3, 8, 128), F32), sin=((3, 8, 128), F32),
    gp=((2, 4, 256, 128), F32), gx=((2, 4, 256, 128), F32), gs=((4, 2, 256, 128), F32), gr=((4, 2, 256, 128), F32),
    ga=((2, 4, 256, 128), F32), gc=((1024, 256), BF16),
    rs=((8, 4, 128), F32),
    dummy=((256, 8, 128), F32),
)


def kernel(rs_hbm, i0_ref, i1_ref, i2_ref, i3_ref, pn_ref, tg_hbm, out_ref, *scratch):
    names = list(SCRATCH)
    ref = dict(zip(names, scratch[: len(names)]))
    tgs, tg_ref, send_sem, recv_sem, load_sem = scratch[len(names) :]
    rs_ref, fo_ref, so_ref = ref["rs"], out_ref.at[0], out_ref.at[1]
    front = lax.axis_index("front")
    side = lax.axis_index("rhs")
    core = front % 2
    chip_y = (front // 2) % 4
    d = front % 8
    z = front // 8
    is_one = core == 1
    stage = Stage()
    drains = []
    cc = [ref["c0"], ref["c1"], ref["c2"], ref["c3"]]
    rb = [ref["rb0"], ref["rb1"], ref["rb2"], ref["rb3"]]
    sd = [ref["sd0"], ref["sd1"], ref["sd2"], ref["sd3"]]
    pc = [None, ref["pc1"], ref["pc2"], ref["pc3"]]
    zz = [z, z % 4, z % 2, 0]
    pair = pl.ds(2 * chip_y, 2)

    def on_one(body):
        pl.when(is_one)(body)

    def on_zero(body):
        pl.when(jnp.logical_not(is_one))(body)

    def put(src, dst, st, to, axis="front"):
        pltpu.make_async_remote_copy(
            src_ref=src, dst_ref=dst, send_sem=send_sem.at[st], recv_sem=recv_sem.at[st],
            device_id={axis: to}, device_id_type=MESH,
        ).start()

    def drain(sem, blocks):
        while blocks:
            some = min(blocks, 256)
            piece = ref["dummy"].at[pl.ds(0, some)]
            pltpu.make_async_copy(piece, piece, sem).wait()
            blocks -= some

    def arrived(st, blocks):
        drain(recv_sem.at[st], blocks)

    def finish_sends(core_number):
        for st_x, zero, one in drains:
            drain(send_sem.at[st_x], one if core_number else zero)

    barrier = pltpu.get_barrier_semaphore()
    masks = list(range(1, 16)) + [8 * m for m in range(2, 8)]
    for mask in masks:
        pl.semaphore_signal(barrier, inc=1, device_id={"front": front ^ mask}, device_id_type=MESH)
    for k in range(1, 4):
        pl.semaphore_signal(barrier, inc=1, device_id={"rhs": side ^ k}, device_id_type=MESH)

    inverse_refs = (i0_ref, i1_ref, i2_ref, i3_ref)

    def load(name):
        t = int(name[1])
        if name[0] == "p":
            return pltpu.make_async_copy(pn_ref.at[t - 1], ref["vp"].at[t - 1], load_sem.at[t + 3])
        return pltpu.make_async_copy(inverse_refs[t], ref[name], load_sem.at[t])

    rs_copy = pltpu.make_async_copy(rs_hbm, rs_ref, load_sem.at[8])
    rs_copy.start()
    tg_copy = pltpu.make_async_copy(tg_hbm, tg_ref, load_sem.at[9])
    tg_copy.start()
    load("v3").start()
    load("p3").start()

    @on_one
    def _():
        load("v2").start()
        load("p2").start()
        load("v1").start()
        load("p1").start()
        load("v0").start()

    rs_copy.wait()
    tg_copy.wait()
    for t in range(TIERS):
        rb[t][zz[t], chip_y, core] = rs_ref[:, t, :]
    lanes = lax.broadcasted_iota(I32, (8, 128), 1)
    own_targets = jnp.full((8, 128), -1, I32)
    for k in range(3):
        for u in range(SLOTS):
            own_targets = jnp.where(lanes == k * 8 + u, tg_ref[k, 0, u], own_targets)
    ref["tgv"][z] = own_targets

    pl.semaphore_wait(barrier, len(masks) + 3)

    st_r3 = stage.take()
    for mask in (4, 5, 2, 3, 6, 7, 1):
        put(rb[3].at[0, chip_y, core], rb[3].at[0, chip_y, core], st_r3, front ^ mask)
    drains.append((st_r3, 7, 7))
    st_tg = stage.take()
    st_rc = stage.take()
    st_rz = [stage.take() for t in range(3)]
    st_w = {name: stage.take() for name in ("w2", "p2", "w1", "p1", "w0")}

    @on_zero
    def _():
        for t in (2, 1, 0):
            put(rb[t].at[zz[t], chip_y, 0], rb[t].at[zz[t], chip_y, 0], st_rc, front ^ 1)
        put(i2_ref, ref["w2"], st_w["w2"], front ^ 1)
        put(pn_ref.at[1], ref["wp"].at[1], st_w["p2"], front ^ 1)
        put(i1_ref, ref["w1"], st_w["w1"], front ^ 1)
        put(pn_ref.at[0], ref["wp"].at[0], st_w["p1"], front ^ 1)
        put(i0_ref, ref["w0"], st_w["w0"], front ^ 1)

    drains.append((st_rc, 3, 0))
    drains.append((st_w["w2"], 256, 0))
    drains.append((st_w["p2"], 128, 0))
    drains.append((st_w["w1"], 512, 0))
    drains.append((st_w["p1"], 128, 0))
    drains.append((st_w["w0"], 1024, 0))

    def prepare_third():
        load("v3").wait()

        def body(e, carry):
            block = ref["v3"][:, pl.ds(pl.multiple_of(e * 128, 128), 128)]
            high = block.astype(BF16)
            cc[3][e, 0:128, :] = high
            cc[3][e, 128:256, :] = (block - high.astype(F32)).astype(BF16)
            return carry

        lax.fori_loop(0, 8, body, 0)
        load("p3").wait()

        def body_panel(u, carry):
            rows = pl.ds(pl.multiple_of(u * 128, 128), 128)
            block = ref["vp"][2, rows, :]
            high = block.astype(BF16)
            pc[3][rows, 0:128] = high
            pc[3][rows, 128:256] = (block - high.astype(F32)).astype(BF16)
            return carry

        lax.fori_loop(0, 8, body_panel, 0)

    def prepare_inverse(t, first, last):
        if first == 0:
            load("v" + str(t)).wait()
            arrived(st_w["w" + str(t)], 16 * BLOCKS[t])

        def body(e, carry):
            columns = pl.ds(pl.multiple_of(e * 128, 128), 128)
            for i, source in ((0, ref["w" + str(t)]), (1, ref["v" + str(t)])):
                block = source[:, columns]
                high = block.astype(BF16)
                cc[t][e, 256 * i : 256 * i + 128, :] = high
                cc[t][e, 256 * i + 128 : 256 * i + 256, :] = (block - high.astype(F32)).astype(BF16)
            return carry

        lax.fori_loop(first, last, body, 0)

    def prepare_panel(t):
        load("p" + str(t)).wait()
        arrived(st_w["p" + str(t)], 128)

        def body(u, carry):
            rows = pl.ds(pl.multiple_of(u * 128, 128), 128)
            for i, source in ((0, ref["wp"]), (1, ref["vp"])):
                block = source[t - 1, rows, :]
                high = block.astype(BF16)
                pc[t][rows, 256 * i : 256 * i + 128] = high
                pc[t][rows, 256 * i + 128 : 256 * i + 256] = (block - high.astype(F32)).astype(BF16)
            return carry

        lax.fori_loop(0, SLOTS, body, 0)

    def target(m, k, u):
        return tgs[z ^ m, 0, k * 8 + u]

    def dense_forward(t):
        def chunk(index):
            x = jnp.concatenate([rb[t][index, j // 2, j % 2] for j in range(8)], axis=1)
            w = jnp.concatenate([cc[t][index * 8 + j] for j in range(8)], axis=1)
            return fold_all(matmul(split_rows(x), w, TRANSPOSED))

        if PLANES[t] == 1:
            return chunk(0)
        return lax.fori_loop(0, PLANES[t], lambda i, total: total + chunk(i), jnp.zeros((8, 256), F32))

    def slots_forward(t, k, m, block_of):
        parts, weights = [], []
        for u in range(SLOTS):
            tag = target(m, k, u)
            live = jnp.where((tag >> 6) == t, 1.0, 0.0).astype(F32)
            parts.append(block_of(u) * live)
            weights.append(cc[t][tag & (BLOCKS[t] - 1)])
        x = jnp.concatenate(parts, axis=1)
        w = jnp.concatenate(weights, axis=1)
        return fold_all(matmul(split_rows(x), w, TRANSPOSED))

    def panel_forward(t, value, out):
        terms = fold_rows(matmul(doubled(value), pc[t][...], TRANSPOSED))
        for u in range(SLOTS):
            out[u // 2, u % 2] = terms[:, u * 128 : (u + 1) * 128]

    def panel_backward(t, picked):
        x = jnp.concatenate([picked[u] for u in range(SLOTS)], axis=1)
        return fold_all(matmul(split_rows(x), pc[t][...], NATURAL))

    def dense_backward(t, value2, first, last):
        def chunk(index, carry):
            w = jnp.concatenate([cc[t][index * 8 + j] for j in range(8)], axis=1)
            terms = fold_rows(matmul(value2, w, NATURAL))
            for j in range(8):
                sd[t][j // 2, index, j % 2] = terms[:, j * 128 : (j + 1) * 128]
            return carry

        if last - first == 1:
            chunk(first, 0)
        else:
            lax.fori_loop(first, last, chunk, 0)

    def slots_backward(t, k, m, value2, out, place):
        weights, lives = [], []
        for u in range(SLOTS):
            tag = target(m, k, u)
            lives.append(jnp.where((tag >> 6) == t, 1.0, 0.0).astype(F32))
            weights.append(cc[t][tag & (BLOCKS[t] - 1)])
        w = jnp.concatenate(weights, axis=1)
        terms = fold_rows(matmul(value2, w, NATURAL))
        for u in range(SLOTS):
            out[u // 2, place, u % 2] = terms[:, u * 128 : (u + 1) * 128] * lives[u]

    def reduce_send(out, into, blocks):
        st = stage.take()
        for k in (2, 1, 3):
            put(out.at[chip_y ^ k], into.at[k], st, front ^ (2 * k))
        drains.append((st, 0, 3 * blocks))
        return st

    def reduced(out, into, index):
        return (out[(chip_y,) + index] + into[(1,) + index]) + (into[(2,) + index] + into[(3,) + index])

    def spread(src, dst, blocks):
        st = stage.take()
        for mask in (4, 2, 6):
            put(src, dst, st, front ^ mask)
        drains.append((st, 0, 3 * blocks))
        return st

    def hand_over(kind, t, value):
        st = st_out[kind][t]
        out, into, own = (ref["fout"], ref["fin"], fo_ref) if kind == 0 else (ref["sout"], ref["sin"], so_ref)
        out[t] = value[0]
        put(out.at[t], into.at[t], st, front ^ 1)
        own[:, t, :] = value[1]

    st_out = [[stage.take() for t in range(3)] for kind in range(2)]
    for kind in range(2):
        for t in range(3):
            drains.append((st_out[kind][t], 0, 1))

    st_rp = [None] * 3

    def plane_gather(t):
        arrived(st_rz[t], 2 * PLANES[t] - 2)
        st_rp[t] = stage.take()
        for mask in (4, 2, 6):
            put(rb[t].at[:, chip_y], rb[t].at[:, chip_y], st_rp[t], front ^ mask)
        drains.append((st_rp[t], 0, 6 * PLANES[t]))

    @on_one
    def _():
        arrived(st_rc, 3)
        put(rb[2].at[z % 2, chip_y], rb[2].at[z % 2, chip_y], st_rz[2], front ^ 8)
        for m in range(1, 8):
            put(ref["tgv"].at[z], ref["tgv"].at[z], st_tg, front ^ (8 * m))
        for t, count in ((1, 4), (0, 8)):
            for m in range(1, count):
                put(rb[t].at[zz[t], chip_y], rb[t].at[zz[t], chip_y], st_rz[t], front ^ (8 * m))

    for t in range(3):
        drains.append((st_rz[t], 0, 2 * PLANES[t] - 2))
    drains.append((st_tg, 0, 7))
    prepare_third()

    @on_one
    def _():
        plane_gather(2)

    arrived(st_r3, 7)
    forward3 = dense_forward(3)
    panel_forward(3, forward3, ref["up3"])
    st_u3 = stage.take()
    for k in (2, 1, 3):
        put(ref["up3"].at[chip_y ^ k], ref["ur3"].at[d], st_u3, (front ^ (2 * k)) | 1)

    @on_zero
    def _():
        put(ref["up3"].at[chip_y], ref["ur3"].at[d], st_u3, front ^ 1)

    drains.append((st_u3, 8, 6))
    fo_ref[:, 3, :] = forward3
    dense_backward(3, doubled(forward3), 0, 1)
    st_d3 = stage.take()
    for mask in (4, 5, 2, 3, 6, 7, 1):
        put(sd[3].at[chip_y ^ (mask >> 1), 0, core ^ (mask & 1)], ref["dr3"].at[mask], st_d3, front ^ mask)
    drains.append((st_d3, 7, 7))

    def combined_partial():
        quarter = pl.ds(pl.multiple_of(side * 256, 256), 256)
        panel_rows = pc[3][quarter, :]
        swapped = jnp.concatenate([panel_rows[:, 128:], panel_rows[:, :128]], axis=1)
        for j in range(8):
            product = matmul(panel_rows, cc[3][j], NATURAL) + matmul(swapped, cc[3][j], NATURAL)
            ref["gp"][j % 2, j // 2] = product

    def split_combined():
        def body(x, carry):
            block = ref["ga"][core, x]
            high = block.astype(BF16)
            rows = pl.ds(pl.multiple_of(x * 256, 256), 256)
            ref["gc"][rows, 0:128] = high
            ref["gc"][rows, 128:256] = (block - high.astype(F32)).astype(BF16)
            return carry

        lax.fori_loop(0, 4, body, 0)

    def third_total():
        arrived(st_d3, 7)
        total = sd[3][chip_y, 0, core]
        for mask in range(1, 8):
            total = total + ref["dr3"][mask]
        return total

    def third_finish(solved3):
        x = jnp.concatenate([ref["pk3"][0, u] + ref["pk3"][1, u] for u in range(SLOTS)], axis=1)
        so_ref[:, 3, :] = solved3 - fold_all(matmul(split_rows(x), ref["gc"][...], NATURAL))

    st_gx = stage.take()
    drains.append((st_gx, 0, 256))
    st_gr = [stage.take(), stage.take()]
    drains.append((st_gr[0], 96, 0))
    drains.append((st_gr[1], 96, 0))
    st_ga = stage.take()
    drains.append((st_ga, 192, 0))
    st_gd = stage.take()
    drains.append((st_gd, 128, 0))
    st_p3 = stage.take()

    @on_zero
    def _():
        combined_partial()
        arrived(st_gx, 256)

        def add_cross(y, carry):
            for c in range(2):
                ref["gs"][y, c] = ref["gp"][c, y] + ref["gx"][c, y]
            return carry

        lax.fori_loop(0, 4, add_cross, 0)

        def combined_send(half):
            rows = pl.ds(128 * half, 128)
            for k in (2, 1, 3):
                put(ref["gs"].at[chip_y ^ k, :, rows], ref["gr"].at[k, :, rows], st_gr[half], front ^ (2 * k))

        arrived(st_out[0][2], 1)
        fo_ref[:, 2, :] = ref["fin"][2]
        combined_send(0)
        arrived(st_out[0][1], 1)
        fo_ref[:, 1, :] = ref["fin"][1]
        combined_send(1)
        solved3 = third_total()
        arrived(st_out[0][0], 1)
        fo_ref[:, 0, :] = ref["fin"][0]
        arrived(st_gr[0], 96)
        arrived(st_gr[1], 96)
        for c in range(2):
            ref["ga"][c, side] = (ref["gs"][chip_y, c] + ref["gr"][1, c]) + (ref["gr"][2, c] + ref["gr"][3, c])
        for k in (2, 1, 3):
            put(ref["ga"].at[:, side], ref["ga"].at[:, side], st_ga, side ^ k, "rhs")
        arrived(st_ga, 192)
        put(ref["ga"].at[1], ref["ga"].at[1], st_gd, front ^ 1)
        split_combined()
        finish_sends(0)
        for t in (0, 1):
            arrived(st_out[1][t], 1)
            so_ref[:, t, :] = ref["sin"][t]
        arrived(st_p3, 16)
        third_finish(solved3)
        arrived(st_out[1][2], 1)
        so_ref[:, 2, :] = ref["sin"][2]

    @on_one
    def _():
        arrived(st_tg, 7)
        targets_copy = pltpu.make_async_copy(ref["tgv"], tgs, load_sem.at[7])
        targets_copy.start()
        prepare_inverse(2, 0, 16)
        targets_copy.wait()
        arrived(st_u3, 14)
        for i in range(2):
            total = ref["up3"][chip_y, i]
            for k in range(1, 8):
                total = total + ref["ur3"][d ^ k, i]
            ref["us3"][i] = total
            ref["s3p"][0, 2 * chip_y + i] = total
        st_s3 = stage.take()
        for mask in (12, 10, 14, 8):
            put(ref["us3"], ref["s3p"].at[1, pair], st_s3, front ^ mask)
        for mask in (4, 2, 6):
            put(ref["us3"], ref["s3p"].at[0, pair], st_s3, front ^ mask)
        drains.append((st_s3, 0, 14))
        st_z3 = stage.take()
        for m in range(2, 8):
            put(ref["us3"], ref["uz3"].at[m], st_z3, front ^ (8 * m))
        drains.append((st_z3, 0, 12))
        plane_gather(1)
        prepare_panel(2)
        arrived(st_rp[2], 12)
        base2 = dense_forward(2)
        combined_partial()
        put(ref["gp"], ref["gx"], st_gx, front ^ 1)
        arrived(st_s3, 14)

        forward = base2
        for m in range(2):
            forward = forward - slots_forward(2, 2, m, lambda u, m=m: ref["s3p"][m, u])
        panel_forward(2, forward, ref["up2"])
        st = reduce_send(ref["up2"], ref["ur2"], 2)
        ref["fk"][2] = forward
        hand_over(0, 2, (forward[:, :128], forward[:, 128:]))
        plane_gather(0)
        arrived(st_z3, 12)
        for m in range(2, 8):
            into = ref["s3q"] if m < 4 else ref["s3r"]
            for i in range(2):
                into[m % 2 if m < 4 else m - 4, 2 * chip_y + i] = ref["uz3"][m, i]
        st_q3 = spread(ref["uz3"].at[pl.ds(2, 2)], ref["s3q"].at[:, pair], 4)
        prepare_inverse(1, 0, 32)
        arrived(st, 6)
        for i in range(2):
            ref["us2"][i] = reduced(ref["up2"], ref["ur2"], (i,))
        st_z2, st_z2b = stage.take(), stage.take()
        for m in (2, 3, 1):
            put(ref["us2"], ref["uz2"].at[m], st_z2, front ^ (8 * m))
        for m in range(4, 8):
            put(ref["us2"], ref["uz2b"].at[m - 4], st_z2b, front ^ (8 * m))
        drains.append((st_z2, 0, 6))
        drains.append((st_z2b, 0, 8))
        prepare_panel(1)
        arrived(st_rp[1], 24)
        base1 = dense_forward(1)
        arrived(st_z2, 6)
        for i in range(2):
            own = ref["us2"][i] + ref["uz2"][1, i]
            other = ref["uz2"][2, i] + ref["uz2"][3, i]
            for h, total in ((0, own), (1, other)):
                ref["st2"][h, i] = total
                ref["s2p"][h, 2 * chip_y + i] = total
        st_s2 = spread(ref["st2"], ref["s2p"].at[:, pair], 4)
        arrived(st_q3, 12)
        for m in range(4):
            src = ref["s3p"].at[m] if m < 2 else ref["s3q"].at[m - 2]
            base1 = base1 - slots_forward(1, 2, m, lambda u, src=src: src[u])
        prepare_inverse(0, 0, 24)
        arrived(st_s2, 12)

        forward = base1
        for h in range(2):
            forward = forward - slots_forward(1, 1, 2 * h, lambda u, h=h: ref["s2p"][h, u])
        panel_forward(1, forward, ref["up1"])
        st = reduce_send(ref["up1"], ref["ur1"], 2)
        ref["fk"][1] = forward
        hand_over(0, 1, (forward[:, :128], forward[:, 128:]))
        arrived(st_z2b, 8)
        for i in range(2):
            for h in range(2):
                total = ref["uz2b"][2 * h, i] + ref["uz2b"][2 * h + 1, i]
                ref["st2b"][h, i] = total
                ref["s2q"][h, 2 * chip_y + i] = total
        st_q2 = spread(ref["st2b"], ref["s2q"].at[:, pair], 4)
        st_r3x = spread(ref["uz3"].at[pl.ds(4, 4)], ref["s3r"].at[:, pair], 8)
        prepare_inverse(0, 24, 64)
        arrived(st, 6)
        for i in range(2):
            ref["us1"][i] = reduced(ref["up1"], ref["ur1"], (i,))
        st_z1 = stage.take()
        for m in (4, 5, 3, 6, 2, 7, 1):
            put(ref["us1"], ref["uz1"].at[m], st_z1, front ^ (8 * m))
        drains.append((st_z1, 0, 14))
        base0 = jnp.zeros((8, 256), F32)
        for h in range(2):
            base0 = base0 - slots_forward(0, 1, 2 * h, lambda u, h=h: ref["s2p"][h, u])
        for m in range(4):
            src = ref["s3p"].at[m] if m < 2 else ref["s3q"].at[m - 2]
            base0 = base0 - slots_forward(0, 2, m, lambda u, src=src: src[u])
        arrived(st_rp[0], 48)
        base0 = base0 + dense_forward(0)
        arrived(st_z1, 14)
        for i in range(2):
            own = ref["us1"][i]
            for m in range(1, 4):
                own = own + ref["uz1"][m, i]
            other = ref["uz1"][4, i]
            for m in range(5, 8):
                other = other + ref["uz1"][m, i]
            for h, total in ((0, own), (1, other)):
                ref["st1"][h, i] = total
                ref["s1p"][h, 2 * chip_y + i] = total
        st_s1 = spread(ref["st1"], ref["s1p"].at[:, pair], 4)
        arrived(st_r3x, 24)
        base0 = lax.fori_loop(
            0, 4, lambda m, total: total - slots_forward(0, 2, m + 4, lambda u: ref["s3r"][m, u]), base0
        )
        arrived(st_q2, 12)
        for h in range(2):
            base0 = base0 - slots_forward(0, 1, 4 + 2 * h, lambda u, h=h: ref["s2q"][h, u])
        arrived(st_s1, 12)

        forward = base0
        for h in range(2):
            forward = forward - slots_forward(0, 0, 4 * h, lambda u, h=h: ref["s1p"][h, u])

        value2 = doubled(forward)
        for h in range(2):
            slots_backward(0, 0, 4 * h, value2, ref["a1"], h)
        st = reduce_send(ref["a1"], ref["ar1"], 4)
        hand_over(0, 0, (forward[:, :128], forward[:, 128:]))
        dense_backward(0, value2, 0, 5)
        arrived(st, 12)
        for h in range(2):
            for i in range(2):
                ref["as1"][h, i] = reduced(ref["a1"], ref["ar1"], (h, i))
        st_z = stage.take()
        for m in (4, 5, 3, 6, 2, 7, 1):
            put(ref["as1"].at[m >> 2], ref["az1"].at[m], st_z, front ^ (8 * m))
        drains.append((st_z, 0, 14))
        dense_backward(0, value2, 5, 8)

        def pick(t, planes, out, place, m, k):
            for u in range(SLOTS):
                tag = target(m, k, u)
                live = jnp.where((tag >> 6) == t, 1.0, 0.0).astype(F32)
                block = sd[t][(tag >> 1) & 3, (tag >> 3) & (planes - 1), tag & 1]
                out[u // 2, place, u % 2] = block * live

        for j in range(12):
            pick(0, 8, ref["n0"], j, 2 * j if j < 4 else j - 4, 1 if j < 4 else 2)
        st_n0 = reduce_send(ref["n0"], ref["nr0"], 24)
        st_d0 = reduce_send(sd[0], ref["dr0"], 16)
        arrived(st_z, 14)
        for i in range(2):
            total = ref["as1"][0, i]
            for m in range(1, 8):
                total = total + ref["az1"][m, i]
            ref["pt1"][i] = total
            ref["pk1"][2 * chip_y + i] = total
        st_p = spread(ref["pt1"], ref["pk1"].at[pair], 2)
        arrived(st_p, 6)

        value2 = doubled(ref["fk"][1] - panel_backward(1, ref["pk1"]))
        for h in range(2):
            slots_backward(1, 1, 2 * h, value2, ref["a2"], h)
        st = reduce_send(ref["a2"], ref["ar2"], 4)
        arrived(st_n0, 72)

        def background_sums(m, carry):
            for i in range(2):
                ref["ns0"][m, 0, i] = reduced(ref["n0"], ref["nr0"], (m // 2, i))
                ref["ns0"][m, 1, i] = reduced(ref["n0"], ref["nr0"], (4 + m, i))
            return carry

        lax.fori_loop(0, 8, background_sums, 0)
        st_nz0 = stage.take()
        for m in (4, 5, 3, 6, 2, 7, 1):
            put(ref["ns0"].at[m], ref["nz0"].at[m], st_nz0, front ^ (8 * m))
        drains.append((st_nz0, 0, 28))
        dense_backward(1, value2, 0, 4)
        for m in range(4):
            pick(1, 4, ref["n1"], m, m, 2)
        st_n1 = reduce_send(ref["n1"], ref["nr1"], 8)
        arrived(st, 12)
        for h in range(2):
            for i in range(2):
                ref["as2"][h, i] = reduced(ref["a2"], ref["ar2"], (h, i))
        st_z = stage.take()
        for m in (2, 3, 1):
            put(ref["as2"].at[m >> 1], ref["az2"].at[m], st_z, front ^ (8 * m))
        drains.append((st_z, 0, 6))
        st_d1 = reduce_send(sd[1], ref["dr1"], 8)

        def plane_totals(st_d, t, into, final, st_f):
            arrived(st_d, 6 * PLANES[t])
            for w in range(PLANES[t]):
                for c in range(2):
                    final[w, c] = reduced(sd[t], into, (w, c))

        plane_totals(st_d0, 0, ref["dr0"], ref["ds0"], None)
        st_dz0 = stage.take()
        for m in (4, 5, 3, 6, 2, 7, 1):
            put(ref["ds0"].at[z ^ m], ref["dz0"].at[m], st_dz0, front ^ (8 * m))
        drains.append((st_dz0, 0, 14))
        arrived(st_nz0, 28)
        for q in range(2):
            for i in range(2):
                total = ref["ns0"][0, q, i]
                for m in range(1, 8):
                    total = total + ref["nz0"][m, q, i]
                ref["t0p"][q, i] = total
        arrived(st_z, 6)
        for i in range(2):
            total = ref["as2"][0, i] + ref["t0p"][0, i]
            for m in range(1, 4):
                total = total + ref["az2"][m, i]
            ref["pt2"][i] = total
            ref["pk2"][2 * chip_y + i] = total
        st_p = spread(ref["pt2"], ref["pk2"].at[pair], 2)
        arrived(st_n1, 24)
        for m in range(4):
            for i in range(2):
                ref["ns1"][m, i] = reduced(ref["n1"], ref["nr1"], (m, i))
        st_nz1 = stage.take()
        for m in (2, 3, 1):
            put(ref["ns1"].at[m], ref["nz1"].at[m], st_nz1, front ^ (8 * m))
        drains.append((st_nz1, 0, 6))
        plane_totals(st_d1, 1, ref["dr1"], ref["ds1"], None)
        st_dz1 = stage.take()
        for m in (2, 3, 1):
            put(ref["ds1"].at[(z ^ m) % 4], ref["dz1"].at[m], st_dz1, front ^ (8 * m))
        drains.append((st_dz1, 0, 6))
        arrived(st_p, 6)

        value2 = doubled(ref["fk"][2] - panel_backward(2, ref["pk2"]))
        for h in range(2):
            slots_backward(2, 2, h, value2, ref["a3"], h)
        st = reduce_send(ref["a3"], ref["ar3"], 4)
        dense_backward(2, value2, 0, 2)
        st_d2 = stage.take()
        for mask in (12, 14, 10, 8, 4, 6, 2):
            put(
                sd[2].at[chip_y ^ ((mask >> 1) & 3), (z ^ (mask >> 3)) % 2],
                ref["dr2"].at[mask >> 1], st_d2, front ^ mask,
            )
        drains.append((st_d2, 0, 14))
        arrived(st_nz1, 6)
        for i in range(2):
            total = ref["ns1"][0, i] + ref["t0p"][1, i]
            for m in range(1, 4):
                total = total + ref["nz1"][m, i]
            ref["t1p"][i] = total
        arrived(st, 12)
        for i in range(2):
            ref["as3"][1, i] = reduced(ref["a3"], ref["ar3"], (1, i))
            total = ref["t1p"][i] + reduced(ref["a3"], ref["ar3"], (0, i))
            ref["as3"][0, i] = total
            ref["pk3"][0, 2 * chip_y + i] = total
        for mask in (12, 13, 10, 11, 14, 15, 8, 9):
            put(ref["as3"].at[1], ref["pk3"].at[1, pair], st_p3, front ^ mask)
        for mask in (4, 5, 2, 3, 6, 7, 1):
            put(ref["as3"].at[0], ref["pk3"].at[0, pair], st_p3, front ^ mask)
        arrived(st_dz0, 14)
        totals = []
        for c in range(2):
            total = ref["ds0"][z, c]
            for m in range(1, 8):
                total = total + ref["dz0"][m, c]
            totals.append(total)
        hand_over(1, 0, totals)
        arrived(st_dz1, 6)
        totals = []
        for c in range(2):
            total = ref["ds1"][z % 4, c]
            for m in range(1, 4):
                total = total + ref["dz1"][m, c]
            totals.append(total)
        hand_over(1, 1, totals)
        arrived(st_d2, 14)
        totals = []
        for c in range(2):
            total = sd[2][chip_y, z % 2, c]
            for m in range(1, 8):
                total = total + ref["dr2"][m, c]
            totals.append(total)
        hand_over(1, 2, totals)
        solved3 = third_total()
        arrived(st_gd, 128)
        split_combined()
        finish_sends(1)
        arrived(st_p3, 14)
        third_finish(solved3)
        drain(send_sem.at[st_p3], 30)

    assert stage.count <= STAGE_COUNT


def shards(right_side, inverse_top, inverse_second, inverse_third, inverse_fourth, panels, targets):
    anywhere = pl.BlockSpec(memory_space=pl.ANY)
    results = pl.pallas_call(
        kernel,
        out_shape=pltpu.VMEM((2,) + right_side.shape, F32),
        in_specs=[anywhere] * 7,
        out_specs=pl.BlockSpec(memory_space=pltpu.VMEM),
        scratch_shapes=[pltpu.VMEM(shape, dtype) for shape, dtype in SCRATCH.values()]
        + [
            pltpu.SMEM((8, 8, 128), I32),
            pltpu.SMEM((3, 1, 8), I32),
            pltpu.SemaphoreType.DMA((STAGE_COUNT,)),
            pltpu.SemaphoreType.DMA((STAGE_COUNT,)),
            pltpu.SemaphoreType.DMA((12,)),
        ],
        compiler_params=pltpu.CompilerParams(
            collective_id=0, has_side_effects=True, vmem_limit_bytes=56 * 2**20
        ),
        name="tiers",
    )(right_side, inverse_top, inverse_second, inverse_third, inverse_fourth, panels, targets)
    return results[0], results[1]


def solution(mesh):
    placed = (
        P("rhs", None, "front"),
        P("front", None),
        P("front", None),
        P("front", None),
        P("front", None),
        P(None, None, "front"),
        P(None, "front", None),
    )
    return jax.shard_map(
        shards,
        mesh=mesh,
        in_specs=placed,
        out_specs=(P("rhs", None, "front"), P("rhs", None, "front")),
        check_vma=False,
    )
```

profile of v0, /device:TPU:1, one launch (start us, length us, event | category | flops | bytes accessed | tf_op | source)
XLA Modules:
  0.0 69.3 jit_solution(18063624061552001223)
XLA Ops:
  0.6 68.0 %tiers.1 = f32[2,8,4,128]{3,2,1,0:T(4,128)S(1)} custom-call(f32[8,4,128]{2,1,0:T(4,128)} %rs_hbm.1, f32[128,8192]{1,0:T(8,128)} %i0_ref.1, f32[128,4096]{1,0:T(8,128)} %i1_ref.1, f32[128,2048]{1,0:T(8,128)} %i2_ref.1, f32[128,1024]{1,0:T(8,128)} %i3_ref.1, f32[3,1024,128]{2,1,0:T(8,128)} %pn_ref.1, s32[3,1,8]{2,1,0:T(1,128)} %tg_hbm.1), custom_call_target="tpu_custom_call" | custom-call | tf_op jit(solution)/shard_map/tiers/pallas_call | solution.py:789
  68.7 0.6 slice_bitcast_fusion
where the time goes:
time: 69.5 us; the launch traced here: 69.3 us
  Pallas kernels  68 us (98%)
    pallas_call x1, Pallas kernels, shards(): pl.pallas_call(kernel, out_shape=pltpu.VMEM((2,) + right_side.shape, F32)...  68 us

commit v1 on v0

--- a/solution.py
+++ b/solution.py
@@ -89,6 +89,7 @@
     gp=((2, 4, 256, 128), F32), gx=((2, 4, 256, 128), F32), gs=((4, 2, 256, 128), F32), gr=((4, 2, 256, 128), F32),
     ga=((2, 4, 256, 128), F32), gc=((1024, 256), BF16),
     rs=((8, 4, 128), F32),
+    wt0=((2048, 512), BF16), wt1=((2048, 512), BF16), wt2=((2048, 512), BF16),
     dummy=((256, 8, 128), F32),
 )
 
@@ -286,6 +287,22 @@
         x = jnp.concatenate(parts, axis=1)
         w = jnp.concatenate(weights, axis=1)
         return fold_all(matmul(split_rows(x), w, TRANSPOSED))
+
+    def turn_slots(t, k, fronts):
+        for h, m in fronts:
+            for u in range(SLOTS):
+                block = cc[t][target(m, k, u) & (BLOCKS[t] - 1)]
+                first = (h * SLOTS + u) * 128
+                ref["wt" + str(t)][first : first + 128, :] = block.T
+
+    def turned_forward(t, k, fronts, sums):
+        parts = []
+        for h, m in fronts:
+            for u in range(SLOTS):
+                live = jnp.where((target(m, k, u) >> 6) == t, 1.0, 0.0).astype(F32)
+                parts.append(sums[h, u] * live)
+        x = jnp.concatenate(parts, axis=1)
+        return fold_all(matmul(split_rows(x), ref["wt" + str(t)][...], NATURAL))
 
     def panel_forward(t, value, out):
         terms = fold_rows(matmul(doubled(value), pc[t][...], TRANSPOSED))
@@ -509,13 +526,12 @@
         prepare_panel(2)
         arrived(st_rp[2], 12)
         base2 = dense_forward(2)
+        turn_slots(2, 2, ((0, 0), (1, 1)))
         combined_partial()
         put(ref["gp"], ref["gx"], st_gx, front ^ 1)
         arrived(st_s3, 14)
 
-        forward = base2
-        for m in range(2):
-            forward = forward - slots_forward(2, 2, m, lambda u, m=m: ref["s3p"][m, u])
+        forward = base2 - turned_forward(2, 2, ((0, 0), (1, 1)), ref["s3p"])
         panel_forward(2, forward, ref["up2"])
         st = reduce_send(ref["up2"], ref["ur2"], 2)
         ref["fk"][2] = forward
@@ -541,6 +557,8 @@
         prepare_panel(1)
         arrived(st_rp[1], 24)
         base1 = dense_forward(1)
+        turn_slots(1, 1, ((0, 0), (1, 2)))
+        prepare_inverse(0, 0, 20)
         arrived(st_z2, 6)
         for i in range(2):
             own = ref["us2"][i] + ref["uz2"][1, i]
@@ -553,12 +571,10 @@
         for m in range(4):
             src = ref["s3p"].at[m] if m < 2 else ref["s3q"].at[m - 2]
             base1 = base1 - slots_forward(1, 2, m, lambda u, src=src: src[u])
-        prepare_inverse(0, 0, 24)
+        prepare_inverse(0, 20, 44)
         arrived(st_s2, 12)
 
-        forward = base1
-        for h in range(2):
-            forward = forward - slots_forward(1, 1, 2 * h, lambda u, h=h: ref["s2p"][h, u])
+        forward = base1 - turned_forward(1, 1, ((0, 0), (1, 2)), ref["s2p"])
         panel_forward(1, forward, ref["up1"])
         st = reduce_send(ref["up1"], ref["ur1"], 2)
         ref["fk"][1] = forward
@@ -571,7 +587,12 @@
                 ref["s2q"][h, 2 * chip_y + i] = total
         st_q2 = spread(ref["st2b"], ref["s2q"].at[:, pair], 4)
         st_r3x = spread(ref["uz3"].at[pl.ds(4, 4)], ref["s3r"].at[:, pair], 8)
-        prepare_inverse(0, 24, 64)
+        prepare_inverse(0, 44, 64)
+        turn_slots(0, 0, ((0, 0), (1, 4)))
+        base0 = jnp.zeros((8, 256), F32)
+        for h in range(2):
+            base0 = base0 - slots_forward(0, 1, 2 * h, lambda u, h=h: ref["s2p"][h, u])
+            base0 = base0 - slots_forward(0, 2, h, lambda u, h=h: ref["s3p"][h, u])
         arrived(st, 6)
         for i in range(2):
             ref["us1"][i] = reduced(ref["up1"], ref["ur1"], (i,))
@@ -579,12 +600,8 @@
         for m in (4, 5, 3, 6, 2, 7, 1):
             put(ref["us1"], ref["uz1"].at[m], st_z1, front ^ (8 * m))
         drains.append((st_z1, 0, 14))
-        base0 = jnp.zeros((8, 256), F32)
-        for h in range(2):
-            base0 = base0 - slots_forward(0, 1, 2 * h, lambda u, h=h: ref["s2p"][h, u])
-        for m in range(4):
-            src = ref["s3p"].at[m] if m < 2 else ref["s3q"].at[m - 2]
-            base0 = base0 - slots_forward(0, 2, m, lambda u, src=src: src[u])
+        for m in range(2):
+            base0 = base0 - slots_forward(0, 2, m + 2, lambda u, m=m: ref["s3q"][m, u])
         arrived(st_rp[0], 48)
         base0 = base0 + dense_forward(0)
         arrived(st_z1, 14)
@@ -608,16 +625,14 @@
             base0 = base0 - slots_forward(0, 1, 4 + 2 * h, lambda u, h=h: ref["s2q"][h, u])
         arrived(st_s1, 12)
 
-        forward = base0
-        for h in range(2):
-            forward = forward - slots_forward(0, 0, 4 * h, lambda u, h=h: ref["s1p"][h, u])
+        forward = base0 - turned_forward(0, 0, ((0, 0), (1, 4)), ref["s1p"])
 
         value2 = doubled(forward)
         for h in range(2):
             slots_backward(0, 0, 4 * h, value2, ref["a1"], h)
         st = reduce_send(ref["a1"], ref["ar1"], 4)
         hand_over(0, 0, (forward[:, :128], forward[:, 128:]))
-        dense_backward(0, value2, 0, 5)
+        dense_backward(0, value2, 0, 7)
         arrived(st, 12)
         for h in range(2):
             for i in range(2):
@@ -626,7 +641,7 @@
         for m in (4, 5, 3, 6, 2, 7, 1):
             put(ref["as1"].at[m >> 2], ref["az1"].at[m], st_z, front ^ (8 * m))
         drains.append((st_z, 0, 14))
-        dense_backward(0, value2, 5, 8)
+        dense_backward(0, value2, 7, 8)
 
         def pick(t, planes, out, place, m, k):
             for u in range(SLOTS):
@@ -638,7 +653,6 @@
         for j in range(12):
             pick(0, 8, ref["n0"], j, 2 * j if j < 4 else j - 4, 1 if j < 4 else 2)
         st_n0 = reduce_send(ref["n0"], ref["nr0"], 24)
-        st_d0 = reduce_send(sd[0], ref["dr0"], 16)
         arrived(st_z, 14)
         for i in range(2):
             total = ref["as1"][0, i]
@@ -666,6 +680,7 @@
         for m in (4, 5, 3, 6, 2, 7, 1):
             put(ref["ns0"].at[m], ref["nz0"].at[m], st_nz0, front ^ (8 * m))
         drains.append((st_nz0, 0, 28))
+        st_d0 = reduce_send(sd[0], ref["dr0"], 16)
         dense_backward(1, value2, 0, 4)
         for m in range(4):
             pick(1, 4, ref["n1"], m, m, 2)
@@ -686,11 +701,6 @@
                 for c in range(2):
                     final[w, c] = reduced(sd[t], into, (w, c))
 
-        plane_totals(st_d0, 0, ref["dr0"], ref["ds0"], None)
-        st_dz0 = stage.take()
-        for m in (4, 5, 3, 6, 2, 7, 1):
-            put(ref["ds0"].at[z ^ m], ref["dz0"].at[m], st_dz0, front ^ (8 * m))
-        drains.append((st_dz0, 0, 14))
         arrived(st_nz0, 28)
         for q in range(2):
             for i in range(2):
@@ -714,6 +724,11 @@
         for m in (2, 3, 1):
             put(ref["ns1"].at[m], ref["nz1"].at[m], st_nz1, front ^ (8 * m))
         drains.append((st_nz1, 0, 6))
+        plane_totals(st_d0, 0, ref["dr0"], ref["ds0"], None)
+        st_dz0 = stage.take()
+        for m in (4, 5, 3, 6, 2, 7, 1):
+            put(ref["ds0"].at[z ^ m], ref["dz0"].at[m], st_dz0, front ^ (8 * m))
+        drains.append((st_dz0, 0, 14))
         plane_totals(st_d1, 1, ref["dr1"], ref["ds1"], None)
         st_dz1 = stage.take()
         for m in (2, 3, 1):

time: 69.5 us -> 66.8 us (0.961)
  Pallas kernels: 68 us -> 65.4 us
    pallas_call x1, Pallas kernels: 68 us -> 65.4 us  [shards(): pl.pallas_call(kernel, out_shape=pltpu.VMEM((2,) + right_side.shape, F32)...]
where the time goes in v1:
time: 66.8 us; the launch traced here: 66.6 us
  Pallas kernels  65.4 us (98%)
    pallas_call x1, Pallas kernels, shards(): pl.pallas_call(kernel, out_shape=pltpu.VMEM((2,) + right_side.shape, F32)...  65.4 us

profile of v1, /device:TPU:1, one launch (start us, length us, event | category | flops | bytes accessed | tf_op | source)
XLA Modules:
  0.0 66.6 jit_solution(8722502415157607865)
XLA Ops:
  0.6 65.4 %tiers.1 = f32[2,8,4,128]{3,2,1,0:T(4,128)S(1)} custom-call(f32[8,4,128]{2,1,0:T(4,128)} %rs_hbm.1, f32[128,8192]{1,0:T(8,128)} %i0_ref.1, f32[128,4096]{1,0:T(8,128)} %i1_ref.1, f32[128,2048]{1,0:T(8,128)} %i2_ref.1, f32[128,1024]{1,0:T(8,128)} %i3_ref.1, f32[3,1024,128]{2,1,0:T(8,128)} %pn_ref.1, s32[3,1,8]{2,1,0:T(1,128)} %tg_hbm.1), custom_call_target="tpu_custom_call" | custom-call | tf_op jit(solution)/shard_map/tiers/pallas_call | solution.py:804
  66.0 0.6 slice_bitcast_fusion

commit v2 on v1

--- a/solution.py
+++ b/solution.py
@@ -523,12 +523,12 @@
             put(ref["us3"], ref["uz3"].at[m], st_z3, front ^ (8 * m))
         drains.append((st_z3, 0, 12))
         plane_gather(1)
+        combined_partial()
+        put(ref["gp"], ref["gx"], st_gx, front ^ 1)
         prepare_panel(2)
         arrived(st_rp[2], 12)
         base2 = dense_forward(2)
         turn_slots(2, 2, ((0, 0), (1, 1)))
-        combined_partial()
-        put(ref["gp"], ref["gx"], st_gx, front ^ 1)
         arrived(st_s3, 14)
 
         forward = base2 - turned_forward(2, 2, ((0, 0), (1, 1)), ref["s3p"])
@@ -536,7 +536,6 @@
         st = reduce_send(ref["up2"], ref["ur2"], 2)
         ref["fk"][2] = forward
         hand_over(0, 2, (forward[:, :128], forward[:, 128:]))
-        plane_gather(0)
         arrived(st_z3, 12)
         for m in range(2, 8):
             into = ref["s3q"] if m < 4 else ref["s3r"]
@@ -554,6 +553,7 @@
             put(ref["us2"], ref["uz2b"].at[m - 4], st_z2b, front ^ (8 * m))
         drains.append((st_z2, 0, 6))
         drains.append((st_z2b, 0, 8))
+        plane_gather(0)
         prepare_panel(1)
         arrived(st_rp[1], 24)
         base1 = dense_forward(1)

time: 66.8 us -> 66.8 us (level)
  no operation moved by 1% of the time
where the time goes in v2:
time: 66.8 us; the launch traced here: 66.6 us
  Pallas kernels  65.3 us (98%)
    pallas_call x1, Pallas kernels, shards(): pl.pallas_call(kernel, out_shape=pltpu.VMEM((2,) + right_side.shape, F32)...  65.3 us

profile of v2, /device:TPU:1, one launch (start us, length us, event | category | flops | bytes accessed | tf_op | source)
XLA Modules:
  0.0 66.6 jit_solution(13211927702430206090)
XLA Ops:
  0.6 65.3 %tiers.1 = f32[2,8,4,128]{3,2,1,0:T(4,128)S(1)} custom-call(f32[8,4,128]{2,1,0:T(4,128)} %rs_hbm.1, f32[128,8192]{1,0:T(8,128)} %i0_ref.1, f32[128,4096]{1,0:T(8,128)} %i1_ref.1, f32[128,2048]{1,0:T(8,128)} %i2_ref.1, f32[128,1024]{1,0:T(8,128)} %i3_ref.1, f32[3,1024,128]{2,1,0:T(8,128)} %pn_ref.1, s32[3,1,8]{2,1,0:T(1,128)} %tg_hbm.1), custom_call_target="tpu_custom_call" | custom-call | tf_op jit(solution)/shard_map/tiers/pallas_call | solution.py:804
  66.0 0.6 slice_bitcast_fusion
